TPU v7x, 32 devices: a whole 2x2x4 slice. The times are simulated.
32 devices in a mesh: geom: 2 (over x), edge: 4 (over y, core), mode: 4 (over z).
Axes of the slice: x: 2, y: 2, z: 4, core: 2. Of those that a mesh axis runs over, the one named last changes fastest.
Arguments:
- basis: bfloat16 [12288, 1024], P(('geom', 'edge'), 'mode'), parts along dimension 0, may hold values from -6 to 6
- motional: bfloat16 [4, 48, 16, 128, 128], P('geom', 'edge'), parts along dimension 0, may hold values from -0.0017089844 to 0.0017089844
- block_cols: int32 [96, 16], P(('geom', 'edge')), parts along dimension 0, may hold values from 0 to 47, as said below
- block_counts: int32 [96], P(('geom', 'edge')), parts along dimension 0, may hold values from 8 to 16, as said below
Outputs:
- reduced: float32 [4, 1024, 1024], P('geom', 'edge', 'mode'), parts along dimension 0
There are 2 independent parts, one for each index of `geom`. A program takes and returns all parts, laid end to end along the dimension named above; each array names one. Nothing has to cross between parts.
Inputs may be any that keep to these rules, and one draw needn't show every extreme that they name: `block_cols`: block row r's live slots hold distinct block columns within 12 blocks of r (at most r + 12, at least r - 12); slot 0 is r itself; slots at or past block_counts[r] hold r. block_counts[r] never exceeds the number of block columns within 12 blocks of r.
All inputs are finite; a program needn't handle non-finite values.
Results may differ from a plain program's by a relative error of at most 0.0029.
Values may be sent and summed in bfloat16 or wider, within the bound.
A program may use at most 64 MiB of HBM per device.

v0:
```python
import jax
import jax.numpy as jnp
from jax import lax
from jax.sharding import PartitionSpec as P


def padded(x, sides, width):
    for axis, dim in sides:
        size, length = (lax.axis_size(axis), x.shape[dim])
        up = [(i, (i + 1) % size) for i in range(size - 1)]
        down = [(j, i) for i, j in up]
        last = lax.slice_in_dim(x, length - width, length, axis=dim)
        initial = lax.slice_in_dim(x, 0, width, axis=dim)
        before = lax.ppermute(last, axis, up)
        after = lax.ppermute(initial, axis, down)
        x = jnp.concatenate([before, x, after], axis=dim)
    return x


def per_device(basis, motional, block_cols, block_counts):
    rows, cols_local = basis.shape
    nbr, nnz = block_cols.shape
    bsize = motional.shape[-1]
    extended = padded(basis, (("edge", 0),), nbr * bsize)
    tiles = extended.reshape(3 * nbr, bsize, cols_local)
    first_block = lax.axis_index("edge") * nbr
    local_cols = block_cols - first_block + nbr
    live = jnp.arange(nnz, dtype=jnp.int32)[None, :] < block_counts[:, None]
    picked = jnp.take(tiles, local_cols, axis=0)
    picked = jnp.where(live[:, :, None, None], picked, jnp.zeros_like(picked))
    work = jnp.einsum("qbkij,bkjm->qbim", motional, picked, preferred_element_type=jnp.float32)
    work = work.astype(jnp.bfloat16).reshape(2, rows, cols_local)
    partial_sum = jnp.einsum(
        "ri,qrj->qij",
        lax.all_gather(basis, "mode", axis=1, tiled=True),
        work,
        preferred_element_type=jnp.float32,
    )
    total = lax.psum(partial_sum, "edge")
    share = total.shape[1] // lax.axis_size("edge")
    return lax.dynamic_slice_in_dim(total, lax.axis_index("edge") * share, share, 1)


def solution(mesh):
    placed = (
        P(("geom", "edge"), "mode"),
        P("geom", "edge", None, None, None),
        P(("geom", "edge"), None),
        P(("geom", "edge")),
    )
    return jax.shard_map(
        per_device, mesh=mesh, in_specs=placed, out_specs=P("geom", "edge", "mode"), check_vma=False
    )
```

profile of v0, /device:TPU:0, one launch (start us, length us, event | category | flops | bytes accessed | tf_op | source)
XLA Modules:
  0.0 138.8 jit_solution(16012564998397765538)
XLA Ops:
  6.5 0.0 all-gather.2.cloned.1.call-start
  6.5 0.7 all-gather.2.cloned.1.call-update
  7.3 0.0 all-reduce.2.cloned.1.call-start
  7.3 2.4 %collective-permute-start = (bf16[1536,256]{1,0:T(8,128)(2,1)}, bf16[1536,256]{1,0:T(8,128)(2,1)S(1)}, u32[]{:S(2)}, u32[]{:S(2)}) collective-permute-start(bf16[1536,256]{1,0:T(8,128)(2,1)} %param.4), channel_id=1, source_target_pairs={{0,4},{4,8},{8,12},{1,5},{5,9},{9,13},{2,6},{6,10},{10,14},{3,7},{... | collective-permute-start | bytes 2359304 | tf_op jit(solution)/shard_map/ppermute | solution.py:14
  9.7 1.3 collective-permute-start.1
  11.0 0.8 compare_and_fusion
  11.8 0.1 reshape.36
  11.9 0.0 collective-permute-done
  11.9 4.4 %collective-permute-done.1 = bf16[1536,256]{1,0:T(8,128)(2,1)} collective-permute-done((bf16[1536,256]{1,0:T(8,128)(2,1)}, bf16[1536,256]{1,0:T(8,128)(2,1)}, u32[]{:S(2)}, u32[]{:S(2)}) %collective-permute-start.1) | collective-permute-done | bytes 786464 | tf_op jit(solution)/shard_map/ppermute | solution.py:15
  16.3 1.5 %pad_maximum_fusion = bf16[4608,256]{1,0:T(8,128)(2,1)S(1)} fusion(bf16[1536,256]{1,0:T(8,128)(2,1)} %collective-permute-done.1, bf16[1536,256]{1,0:T(8,128)(2,1)} %param.4, bf16[1536,256]{1,0:T(8,128)(2,1)S(1)} %collective-permute-done), kind=kLoop, calls=%fused_computation.13 | loop fusion | flops 7077888 | bytes 4718592 | tf_op jit(solution)/shard_map/concatenate | solution.py:16
  17.9 8.2 %gather_fusion = bf16[192,128,256]{2,1,0:T(8,128)(2,1)} fusion(bf16[36,128,256]{2,1,0:T(8,128)(2,1)S(1)} %bitcast.27, s32[1024]{0:T(1024)S(1)} %pad_clamp_fusion), kind=kCustom, calls=%fused_computation | custom fusion | bytes 25166592 | tf_op jit(solution)/shard_map/jit(_take)/gather | solution.py:29
  26.1 10.5 %fusion.18 = bf16[2,12,128,256]{3,2,0,1:T(8,128)(2,1)S(1)} fusion(bf16[2,12,16,128,128]{4,3,2,1,0:T(8,128)(2,1)} %param.5, bf16[12,16,128,256]{3,2,1,0:T(8,128)(2,1)} %bitcast.28, pred[12,16]{1,0:T(8,128)(4,1)S(1)} %get-tuple-element.5, pred[12,16]{1,0:T(8,128)(4,1)S(1)} %get-tuple-element.7), kind=kOutput, calls=%fused_computation.15 | convolution fusion | flops 3234594816 | bytes 26739072 | tf_op jit(solution)/shard_map/qbkij,bkjm->qbim/dot_general | solution.py:31
  36.5 0.1 copy.8
  36.7 38.4 %all-gather.2.cloned.1.call-done = bf16[1536,1024]{1,0:T(8,128)(2,1)} async-done(((bf16[1536,256]{1,0:T(8,128)(2,1)}), bf16[1536,1024]{1,0:T(8,128)(2,1)}) %all-gather.2.cloned.1.call-update) | async-done | bytes 3145744 | tf_op jit(solution)/shard_map/all_gather | solution.py:35
  75.1 5.0 %fusion.15 = f32[2,1024,256]{1,2,0:T(8,128)} fusion(bf16[2,1536,256]{2,1,0:T(8,128)(2,1)S(1)} %bitcast.29, bf16[1536,1024]{1,0:T(8,128)(2,1)} %all-gather.2.cloned.1.call-done), kind=kOutput, calls=%fused_computation.14 | convolution fusion | flops 1610612736 | bytes 6815744 | tf_op jit(solution)/shard_map/ri,qrj->qij/dot_general | solution.py:33
  80.1 0.0 all-reduce.2.cloned.1.call-update
  80.2 49.7 %all-reduce.2.cloned.1.call-done = f32[2,1024,256]{1,2,0:T(8,128)} async-done(((f32[2,1024,256]{1,2,0:T(8,128)}), f32[2,1024,256]{1,2,0:T(8,128)}) %all-reduce.2.cloned.1.call-update) | async-done | bytes 2097168 | tf_op jit(solution)/shard_map/psum | solution.py:39
  129.9 1.1 constant_dynamic-slice_fusion
  130.9 1.0 copy.10
  (1 shorter events, 0.0 us)
Async XLA Ops:
  6.5 68.5 %all-gather.2.cloned.1.call-start = ((), (), s32[]{:S(2)}) async-start(), calls=%async_computation | async-start | bytes 3932160 | tf_op jit(solution)/shard_map/all_gather | solution.py:35
  7.3 122.6 %all-reduce.2.cloned.1.call-start = ((), (), s32[]{:S(2)}) async-start(), calls=%async_computation.1 | async-start | bytes 4194304 | tf_op jit(solution)/shard_map/psum | solution.py:39
  7.3 4.6 %collective-permute-start = (bf16[1536,256]{1,0:T(8,128)(2,1)}, bf16[1536,256]{1,0:T(8,128)(2,1)S(1)}, u32[]{:S(2)}, u32[]{:S(2)}) collective-permute-start(bf16[1536,256]{1,0:T(8,128)(2,1)} %param.4), channel_id=1, source_target_pairs={{0,4},{4,8},{8,12},{1,5},{5,9},{9,13},{2,6},{6,10},{10,14},{3,7},{... | collective-permute-start | bytes 2359304 | tf_op jit(solution)/shard_map/ppermute | solution.py:14
  9.7 6.6 %collective-permute-start.1 = (bf16[1536,256]{1,0:T(8,128)(2,1)}, bf16[1536,256]{1,0:T(8,128)(2,1)}, u32[]{:S(2)}, u32[]{:S(2)}) collective-permute-start(bf16[1536,256]{1,0:T(8,128)(2,1)} %param.4), channel_id=1, source_target_pairs={{4,0},{8,4},{12,8},{5,1},{9,5},{13,9},{6,2},{10,6},{14,10},{7,3},{... | collective-permute-start | bytes 2359304 | tf_op jit(solution)/shard_map/ppermute | solution.py:15
Sparse Core Ops, SparseCore 0:
  8.9 66.1 all-gather.1
  80.3 49.5 all-reduce.1
where the time goes:
time: 139 us
  waiting for transfers between devices  93.2 us (67%)
  matrix products  15.5 us (11%)
  between operations  13.5 us (10%)
  local copies, waits for them, and re-layouts  10.5 us (8%)
  starting transfers between devices  3.74 us (3%)
  other arithmetic  2.31 us (2%)
    psum x1, waiting for transfers between devices, per_device(): total = lax.psum(partial_sum, 'edge')  49.7 us
    all_gather x1, waiting for transfers between devices, per_device(): lax.all_gather(basis, 'mode', axis=1, tiled=True)  38.4 us
    dot_general x1, matrix products, per_device(): jnp.einsum('qbkij,bkjm->qbim', motional, picked, preferred_element_type=j...  10.5 us
    gather x1, local copies, waits for them, and re-layouts, per_device(): picked = jnp.take(tiles, local_cols, axis=0)  8.2 us
    dot_general x1, matrix products, per_device(): jnp.einsum('ri,qrj->qij', lax.all_gather(basis, 'mode', axis=1, tiled=Tru...  5.05 us
    ppermute x1, waiting for transfers between devices, padded(): after = lax.ppermute(initial, axis, down)  4.43 us
  transfers between devices with their start and end apart: 4, of which 3 were waited for; matrix products, arithmetic and copies ran while one was open for 15% of the time, Pallas kernels for 0%

commit v1 on v0

--- a/solution.py
+++ b/solution.py
@@ -36,7 +36,7 @@
         work,
         preferred_element_type=jnp.float32,
     )
-    total = lax.psum(partial_sum, "edge")
+    total = jnp.sum(lax.all_gather(partial_sum, "edge"), axis=0)
     share = total.shape[1] // lax.axis_size("edge")
     return lax.dynamic_slice_in_dim(total, lax.axis_index("edge") * share, share, 1)
 

time: 139 us -> 150 us (1.079)
  waiting for transfers between devices: 93.2 us -> 99.1 us
  other arithmetic: 2.31 us -> 6.51 us
  local copies, waits for them, and re-layouts: 10.5 us -> 12.2 us
    all_gather x0 -> x1, waiting for transfers between devices: none -> 56.6 us  [per_device(): total = jnp.sum(lax.all_gather(partial_sum, 'edge'), axis=0)]
    psum x1 -> x0, waiting for transfers between devices: 49.7 us -> none  [per_device(): total = lax.psum(partial_sum, 'edge')]
    reduce_sum x0 -> x1, other arithmetic: none -> 4.21 us  [per_device(): total = jnp.sum(lax.all_gather(partial_sum, 'edge'), axis=0)]
    transpose x0 -> x1, local copies, waits for them, and re-layouts: none -> 1.86 us  [per_device(): jnp.einsum('ri,qrj->qij', lax.all_gather(basis, 'mode', axis=1, tiled=Tru...]
where the time goes in v1:
time: 150 us
  waiting for transfers between devices  99.1 us (66%)
  matrix products  14.7 us (10%)
  between operations  13.5 us (9%)
  local copies, waits for them, and re-layouts  12.2 us (8%)
  other arithmetic  6.51 us (4%)
  starting transfers between devices  3.74 us (2%)
    all_gather x1, waiting for transfers between devices, per_device(): total = jnp.sum(lax.all_gather(partial_sum, 'edge'), axis=0)  56.6 us
    all_gather x1, waiting for transfers between devices, per_device(): lax.all_gather(basis, 'mode', axis=1, tiled=True)  37.3 us
    dot_general x1, matrix products, per_device(): jnp.einsum('qbkij,bkjm->qbim', motional, picked, preferred_element_type=j...  10.5 us
    gather x1, local copies, waits for them, and re-layouts, per_device(): picked = jnp.take(tiles, local_cols, axis=0)  8.2 us
    ppermute x1, waiting for transfers between devices, padded(): after = lax.ppermute(initial, axis, down)  4.43 us
    reduce_sum x1, other arithmetic, per_device(): total = jnp.sum(lax.all_gather(partial_sum, 'edge'), axis=0)  4.21 us
    dot_general x1, matrix products, per_device(): jnp.einsum('ri,qrj->qij', lax.all_gather(basis, 'mode', axis=1, tiled=Tru...  4.17 us
  transfers between devices with their start and end apart: 4, of which 3 were waited for; matrix products, arithmetic and copies ran while one was open for 15% of the time, Pallas kernels for 0%

profile of v1, /device:TPU:0, one launch (start us, length us, event | category | flops | bytes accessed | tf_op | source)
XLA Modules:
  0.0 149.6 jit_solution(8080490778399640467)
XLA Ops:
  6.5 0.0 all-gather.4.cloned.1.call-start
  6.5 0.7 all-gather.4.cloned.1.call-update
  7.3 0.0 all-gather.6.cloned.1.call-start
  7.3 2.4 %collective-permute-start = (bf16[1536,256]{1,0:T(8,128)(2,1)}, bf16[1536,256]{1,0:T(8,128)(2,1)S(1)}, u32[]{:S(2)}, u32[]{:S(2)}) collective-permute-start(bf16[1536,256]{1,0:T(8,128)(2,1)} %param.4), channel_id=1, source_target_pairs={{0,4},{4,8},{8,12},{1,5},{5,9},{9,13},{2,6},{6,10},{10,14},{3,7},{... | collective-permute-start | bytes 2359304 | tf_op jit(solution)/shard_map/ppermute | solution.py:14
  9.7 1.3 collective-permute-start.1
  11.0 0.8 compare_and_fusion
  11.8 0.1 reshape.36
  11.9 0.0 collective-permute-done
  11.9 4.4 %collective-permute-done.1 = bf16[1536,256]{1,0:T(8,128)(2,1)} collective-permute-done((bf16[1536,256]{1,0:T(8,128)(2,1)}, bf16[1536,256]{1,0:T(8,128)(2,1)}, u32[]{:S(2)}, u32[]{:S(2)}) %collective-permute-start.1) | collective-permute-done | bytes 786464 | tf_op jit(solution)/shard_map/ppermute | solution.py:15
  16.3 1.5 %pad_maximum_fusion = bf16[4608,256]{1,0:T(8,128)(2,1)S(1)} fusion(bf16[1536,256]{1,0:T(8,128)(2,1)} %collective-permute-done.1, bf16[1536,256]{1,0:T(8,128)(2,1)} %param.4, bf16[1536,256]{1,0:T(8,128)(2,1)S(1)} %collective-permute-done), kind=kLoop, calls=%fused_computation.13 | loop fusion | flops 7077888 | bytes 4718592 | tf_op jit(solution)/shard_map/concatenate | solution.py:16
  17.9 8.2 %gather_fusion = bf16[192,128,256]{2,1,0:T(8,128)(2,1)} fusion(bf16[36,128,256]{2,1,0:T(8,128)(2,1)S(1)} %bitcast.28, s32[1024]{0:T(1024)S(1)} %pad_clamp_fusion), kind=kCustom, calls=%fused_computation | custom fusion | bytes 25166592 | tf_op jit(solution)/shard_map/jit(_take)/gather | solution.py:29
  26.1 10.5 %fusion.18 = bf16[2,12,128,256]{3,2,0,1:T(8,128)(2,1)S(1)} fusion(bf16[2,12,16,128,128]{4,3,2,1,0:T(8,128)(2,1)} %param.5, bf16[12,16,128,256]{3,2,1,0:T(8,128)(2,1)} %bitcast.29, pred[12,16]{1,0:T(8,128)(4,1)S(1)} %get-tuple-element.5, pred[12,16]{1,0:T(8,128)(4,1)S(1)} %get-tuple-element.7), kind=kOutput, calls=%fused_computation.15 | convolution fusion | flops 3234594816 | bytes 26739072 | tf_op jit(solution)/shard_map/qbkij,bkjm->qbim/dot_general | solution.py:31
  36.6 1.3 copy.10
  37.8 37.3 %all-gather.4.cloned.1.call-done = bf16[1536,1024]{1,0:T(8,128)(2,1)} async-done(((bf16[1536,256]{1,0:T(8,128)(2,1)}), bf16[1536,1024]{1,0:T(8,128)(2,1)}) %all-gather.4.cloned.1.call-update) | async-done | bytes 3145744 | tf_op jit(solution)/shard_map/all_gather | solution.py:35
  75.1 4.2 %fusion.15 = f32[2,1024,256]{1,2,0:T(8,128)S(1)} fusion(bf16[2,1536,256]{2,1,0:T(8,128)(2,1)} %bitcast.31, bf16[1536,1024]{1,0:T(8,128)(2,1)} %all-gather.4.cloned.1.call-done), kind=kOutput, calls=%fused_computation.14 | convolution fusion | flops 1610612736 | bytes 6815744 | tf_op jit(solution)/shard_map/ri,qrj->qij/dot_general | solution.py:33
  79.2 1.9 %copy.12 = f32[2,1024,256]{2,1,0:T(8,128)} copy(f32[2,1024,256]{1,2,0:T(8,128)S(1)} %fusion.15) | data formatting | bytes 4194304 | tf_op jit(solution)/shard_map/ri,qrj->qij/transpose | solution.py:33
  81.1 0.0 all-gather.6.cloned.1.call-update
  81.1 56.6 %all-gather.6.cloned.1.call-done = f32[8,1024,256]{2,1,0:T(8,128)} async-done(((f32[2,1024,256]{2,1,0:T(8,128)}), f32[8,1024,256]{2,1,0:T(8,128)}) %all-gather.6.cloned.1.call-update) | async-done | bytes 8388624 | tf_op jit(solution)/shard_map/all_gather | solution.py:39
  137.8 4.2 %reduce_sum.9 = f32[2,1024,256]{2,1,0:T(8,128)S(1)} reduce(f32[4,2,1024,256]{3,2,1,0:T(8,128)} %bitcast.30, f32[]{:T(128)} %constant.31.clone.1), dimensions={0}, to_apply=%region_0.1 | reduce | flops 1572864 | bytes 10485764 | tf_op jit(solution)/shard_map/reduce_sum | solution.py:39
  142.0 0.8 constant_dynamic-slice_fusion
  (1 shorter events, 0.0 us)
Async XLA Ops:
  6.5 68.5 %all-gather.4.cloned.1.call-start = ((), (), s32[]{:S(2)}) async-start(), calls=%async_computation | async-start | bytes 3932160 | tf_op jit(solution)/shard_map/all_gather | solution.py:35
  7.3 130.5 %all-gather.6.cloned.1.call-start = ((), (), s32[]{:S(2)}) async-start(), calls=%async_computation.1 | async-start | bytes 10485760 | tf_op jit(solution)/shard_map/all_gather | solution.py:39
  7.3 4.6 %collective-permute-start = (bf16[1536,256]{1,0:T(8,128)(2,1)}, bf16[1536,256]{1,0:T(8,128)(2,1)S(1)}, u32[]{:S(2)}, u32[]{:S(2)}) collective-permute-start(bf16[1536,256]{1,0:T(8,128)(2,1)} %param.4), channel_id=1, source_target_pairs={{0,4},{4,8},{8,12},{1,5},{5,9},{9,13},{2,6},{6,10},{10,14},{3,7},{... | collective-permute-start | bytes 2359304 | tf_op jit(solution)/shard_map/ppermute | solution.py:14
  9.7 6.6 %collective-permute-start.1 = (bf16[1536,256]{1,0:T(8,128)(2,1)}, bf16[1536,256]{1,0:T(8,128)(2,1)}, u32[]{:S(2)}, u32[]{:S(2)}) collective-permute-start(bf16[1536,256]{1,0:T(8,128)(2,1)} %param.4), channel_id=1, source_target_pairs={{4,0},{8,4},{12,8},{5,1},{9,5},{13,9},{6,2},{10,6},{14,10},{7,3},{... | collective-permute-start | bytes 2359304 | tf_op jit(solution)/shard_map/ppermute | solution.py:15
Sparse Core Ops, SparseCore 0:
  8.9 66.1 all-gather.3
  81.2 56.4 all-gather.5
